TPU v7x, 32 devices: a whole 2x2x4 slice. The times are simulated.
32 devices in a mesh: expert: 16 (over z, y, x), dp: 2 (over core).
Axes of the slice: x: 2, y: 2, z: 4, core: 2. Of those that a mesh axis runs over, the one named last changes fastest.
Arguments:
- tokens: bfloat16 [4096, 2048], P(('dp', 'expert')), parts along dimension 0, may hold values from -6 to 6
- logits: float32 [4096, 16], P(('dp', 'expert')), parts along dimension 0, may hold values from -4 to 350
- weights: bfloat16 [16, 2048, 1024], P('expert'), may hold values from -0.125 to 0.125
- router_weight: bfloat16 [2048, 16], replicated, may hold values from -0.125 to 0.125
- expert_picks: int32 [32, 256], P(('dp', 'expert')), parts along dimension 0, may hold values from 0 to 2047, as said below
- cotangent: bfloat16 [32, 256, 1024], P(('dp', 'expert')), parts along dimension 0, may hold values from -1.5 to 1.5
Outputs:
- token_grad: bfloat16 [4096, 2048], P(('dp', 'expert')), parts along dimension 0
- weight_grad: bfloat16 [32, 2048, 1024], P(('dp', 'expert')), parts along dimension 0
- router_grad: float32 [4096, 16], P(('dp', 'expert')), parts along dimension 0
There are 2 independent parts, one for each index of `dp`. A program takes and returns all parts, laid end to end along the dimension named above; an argument that names none is the same for every part. Nothing has to cross between parts.
Inputs may be any that keep to these rules, and one draw needn't show every extreme that they name: `expert_picks`: each expert's list is ascending and names no token twice. Among the tokens of one device (indices k * 128 to (k + 1) * 128 - 1) an expert takes at most 32, and in every draw each expert takes exactly 32 from some devices' tokens.
All inputs are finite; a program needn't handle non-finite values.
Results may differ from a plain program's by a relative error of at most 0.0062.
Values may be sent and summed in bfloat16 or wider, within the bound.
A program may use at most 64 MiB of HBM per device.

v0:
```python
import jax
import jax.numpy as jnp
from jax import lax
from jax.sharding import PartitionSpec as P


def local(tokens, logits, weights, router_weight, expert_picks, cotangent):
    experts = lax.axis_size("expert")
    tok_rows = tokens.shape[0]
    width = tokens.shape[1]
    capacity = expert_picks.shape[1]
    slot_most = 2 * capacity // experts
    slot_total = experts * slot_most
    device_index = lax.axis_index("expert")
    wanted = expert_picks[0]
    owners = wanted // tok_rows
    owner_ids = jnp.arange(experts, dtype=jnp.int32)
    owner_hot = (owners[:, None] == owner_ids[None, :]).astype(jnp.int32)
    counts = jnp.sum(owner_hot, axis=0)
    starts = jnp.cumsum(counts) - counts
    offset = jnp.sum(owner_hot * starts[None, :], axis=1)
    placed = owners * slot_most + jnp.arange(capacity, dtype=jnp.int32) - offset
    all_lists = lax.all_gather(expert_picks, "expert", axis=0, tiled=True)
    slice_low = device_index * tok_rows
    in_slice = (all_lists >= slice_low) & (all_lists < slice_low + tok_rows)
    first_pos = jnp.sum((all_lists < slice_low).astype(jnp.int32), axis=1)
    in_count = jnp.sum(in_slice.astype(jnp.int32), axis=1)
    columns = jnp.arange(slot_most, dtype=jnp.int32)
    positions = jnp.minimum(first_pos[:, None] + columns[None, :], capacity - 1)
    located = jnp.take_along_axis(all_lists, positions, axis=1) - slice_low
    requested = jnp.where(columns[None, :] < in_count[:, None], located, -1)
    filled = requested >= 0
    flat_rows = jnp.maximum(requested, 0).reshape(slot_total)
    gate_probs = jax.nn.softmax(logits, axis=-1)
    send_rows = jnp.take(tokens, flat_rows, axis=0).reshape(experts, slot_most, width)
    send_rows = jnp.where(filled[:, :, None], send_rows, jnp.zeros((), jnp.bfloat16))
    prob_rows = jnp.take(gate_probs, flat_rows, axis=0).reshape(experts, slot_most, experts)
    identity = jnp.eye(experts, dtype=jnp.float32)
    send_gate = jnp.einsum("ejk,ek->ej", prob_rows, identity)
    send_gate = jnp.where(filled, send_gate, 0.0).astype(jnp.bfloat16)
    weight = weights[0]
    upstream = cotangent[0]
    got_rows, got_gate = (
        lax.all_to_all(send_rows, "expert", split_axis=0, concat_axis=0, tiled=True),
        lax.all_to_all(send_gate, "expert", split_axis=0, concat_axis=0, tiled=True),
    )
    picked_rows = jnp.take(got_rows.reshape(slot_total, width), placed, axis=0)
    gate_vals = jnp.take(got_gate.reshape(slot_total), placed).astype(jnp.float32)
    active = jnp.dot(picked_rows, weight, preferred_element_type=jnp.float32)
    gate_grad = jnp.sum(upstream.astype(jnp.float32) * active, axis=1).astype(jnp.bfloat16)
    back_gate = (
        jnp.zeros((slot_total,), jnp.bfloat16).at[placed].set(gate_grad).reshape(experts, slot_most)
    )
    scaled = (gate_vals[:, None] * upstream.astype(jnp.float32)).astype(jnp.bfloat16)
    weight_grad = lax.dot_general(
        picked_rows, scaled, (((0,), (0,)), ((), ())), preferred_element_type=jnp.float32
    ).astype(jnp.bfloat16)
    row_grad = lax.dot_general(
        scaled, weight, (((1,), (1,)), ((), ())), preferred_element_type=jnp.float32
    ).astype(jnp.bfloat16)
    back_rows = (
        jnp.zeros((slot_total, width), jnp.bfloat16)
        .at[placed]
        .set(row_grad)
        .reshape(experts, slot_most, width)
    )
    got_row_grad, got_gate_grad = (
        lax.all_to_all(back_rows, "expert", split_axis=0, concat_axis=0, tiled=True),
        lax.all_to_all(back_gate, "expert", split_axis=0, concat_axis=0, tiled=True),
    )
    token_ids = jnp.arange(tok_rows, dtype=jnp.int32)
    selector = (token_ids[:, None] == requested.reshape(slot_total)[None, :]).astype(jnp.bfloat16)
    expert_part = jnp.dot(
        selector, got_row_grad.reshape(slot_total, width), preferred_element_type=jnp.float32
    )
    matches = (token_ids[:, None, None] == requested[None, :, :]).astype(jnp.float32)
    score_grad = jnp.einsum("tej,ej->te", matches, got_gate_grad.astype(jnp.float32))
    inner_sum = jnp.sum(gate_probs * score_grad, axis=1, keepdims=True)
    logit_grad = (gate_probs * (score_grad - inner_sum)).astype(jnp.bfloat16)
    router_part = lax.dot_general(
        logit_grad, router_weight, (((1,), (1,)), ((), ())), preferred_element_type=jnp.float32
    )
    token_grad = (expert_part + router_part).astype(jnp.bfloat16)
    router_grad = lax.psum_scatter(
        lax.dot_general(
            tokens, logit_grad, (((0,), (0,)), ((), ())), preferred_element_type=jnp.float32
        ),
        "expert",
        scatter_dimension=0,
        tiled=True,
    )
    return (token_grad, weight_grad[None], router_grad)


def solution(mesh):
    in_specs = (
        P(("dp", "expert"), None),
        P(("dp", "expert"), None),
        P("expert", None, None),
        P(),
        P(("dp", "expert"), None),
        P(("dp", "expert"), None, None),
    )
    out_specs = (
        P(("dp", "expert"), None),
        P(("dp", "expert"), None, None),
        P(("dp", "expert"), None),
    )
    return jax.shard_map(local, mesh=mesh, in_specs=in_specs, out_specs=out_specs, check_vma=False)
```

profile of v0, /device:TPU:0, one launch (start us, length us, event | category | flops | bytes accessed | tf_op | source)
XLA Modules:
  0.0 239.1 jit_solution(15871713526536447228)
XLA Ops:
  7.2 42.8 %all-gather = s32[16,1,256]{2,1,0:T(1,128)S(1)} all-gather(s32[1,1,256]{2,1,0:T(1,128)} %bitcast.95), channel_id=1, replica_groups=mesh['expert'=16,'dp'=2] {'expert'}, dimensions={0}, use_global_device_ids=true | all-gather | bytes 17408 | tf_op jit(solution)/shard_map/all_gather | solution.py:23
  50.3 4.5 %gather_fusion.4 = s32[512]{0:T(512)S(1)} fusion(s32[16,256]{1,0:T(8,128)S(1)} %bitcast.86, s32[512]{0:T(512)S(1)} %reshape.529), kind=kCustom, calls=%fused_computation.4 | custom fusion | bytes 8192 | tf_op jit(solution)/shard_map/jit(take_along_axis)/gather | solution.py:30
  55.3 2.5 %gather_fusion.2 = bf16[512,2048]{1,0:T(8,128)(2,1)S(1)} fusion(bf16[128,2048]{1,0:T(8,128)(2,1)S(1)} %copy-done, s32[1024]{0:T(1024)S(1)} %pad_clamp_fusion.1), kind=kCustom, calls=%fused_computation.2 | custom fusion | bytes 4196352 | tf_op jit(solution)/shard_map/jit(_take)/gather | solution.py:35
  57.8 1.6 select_select_fusion
  59.5 3.9 %all-to-all-start.2 = ((bf16[16,32,2048]{2,1,0:T(8,128)(2,1)}), bf16[16,32,2048]{2,1,0:T(8,128)(2,1)S(1)}, u32[]{:S(2)}, u32[]{:S(2)}) async-start(bf16[16,32,2048]{2,1,0:T(8,128)(2,1)} %select_select_fusion), calls=%async_computation.2 | async-start | bytes 4194304 | tf_op jit(solution)/shard_map/all_to_all | solution.py:44
  64.0 38.0 %all-to-all-done.2 = bf16[16,32,2048]{2,1,0:T(8,128)(2,1)S(1)} async-done(((bf16[16,32,2048]{2,1,0:T(8,128)(2,1)}), bf16[16,32,2048]{2,1,0:T(8,128)(2,1)S(1)}, u32[]{:S(2)}, u32[]{:S(2)}) %all-to-all-start.2) | async-done | bytes 2097184 | tf_op jit(solution)/shard_map/all_to_all | solution.py:44
  102.0 2.3 gather_fusion.3
  104.3 3.9 %fusion.12 = bf16[256]{0:T(256)(128)(2,1)S(1)} fusion(bf16[1,2048,1024]{2,1,0:T(8,128)(2,1)} %param.8, bf16[1,256,1024]{2,1,0:T(8,128)(2,1)S(1)} %copy-done.4, bf16[256,2048]{1,0:T(8,128)(2,1)} %gather_fusion.3, pred[256]{0:T(512)(128)(4,1)S(1)} %compare_and_fusion), kind=kOutput, calls=%fused_computation.21 | convolution fusion | flops 1075052288 | bytes 5767936 | tf_op jit(solution)/shard_map/dot_general | solution.py:49
  108.2 2.2 scatter_custom_fusion.1
  110.4 0.7 all_to_all.27
  111.1 7.4 %all-to-all-start.3 = ((bf16[16,1,32]{2,1,0:T(2,128)(2,1)}), bf16[16,1,32]{2,1,0:T(2,128)(2,1)S(1)}, u32[]{:S(2)}, u32[]{:S(2)}) async-start(bf16[16,1,32]{2,1,0:T(2,128)(2,1)} %all_to_all.27), calls=%async_computation.3 | async-start | bytes 16384 | tf_op jit(solution)/shard_map/all_to_all | solution.py:69
  118.5 7.2 %all-to-all-done.3 = bf16[16,1,32]{2,1,0:T(2,128)(2,1)S(1)} async-done(((bf16[16,1,32]{2,1,0:T(2,128)(2,1)}), bf16[16,1,32]{2,1,0:T(2,128)(2,1)S(1)}, u32[]{:S(2)}, u32[]{:S(2)}) %all-to-all-start.3) | async-done | bytes 1056 | tf_op jit(solution)/shard_map/all_to_all | solution.py:69
  126.3 1.3 gather_fusion
  127.9 9.9 %all_to_all.32 = bf16[16,1,32]{2,1,0:T(2,128)(2,1)S(1)} all-to-all(bf16[16,1,32]{2,1,0:T(2,128)(2,1)S(1)} %copy.31), channel_id=1, replica_groups=mesh['expert'=16,'dp'=2] {'expert'}, dimensions={0} | all-to-all | bytes 2048 | tf_op jit(solution)/shard_map/all_to_all | solution.py:45
  137.9 1.9 gather_fusion.1
  139.8 3.5 %fusion.4 = bf16[256,2048]{1,0:T(8,128)(2,1)S(1)} fusion(bf16[1,2048,1024]{2,1,0:T(8,128)(2,1)} %param.8, bf16[1,256,1024]{2,1,0:T(8,128)(2,1)S(1)} %copy-done.4, f32[256]{0:T(256)S(1)} %select_convert_fusion.1), kind=kOutput, calls=%fused_computation.12 | convolution fusion | flops 1075052544 | bytes 5768192 | tf_op jit(solution)/shard_map/dot_general | solution.py:58
  143.4 3.7 %scatter_custom_fusion = bf16[512,2048]{1,0:T(8,128)(2,1)} fusion(s32[256]{0:T(256)S(1)} %bitcast.103, bf16[256,2048]{1,0:T(8,128)(2,1)S(1)} %fusion.4, bf16[]{:T(256)} %constant.103.clone.1), kind=kCustom, calls=%fused_computation.25 | custom fusion | bytes 2097154 | tf_op jit(solution)/shard_map/scatter | solution.py:64
  147.1 3.7 %all-to-all-start.1 = ((bf16[16,32,2048]{2,1,0:T(8,128)(2,1)}), bf16[16,32,2048]{2,1,0:T(8,128)(2,1)S(1)}, u32[]{:S(2)}, u32[]{:S(2)}) async-start(bf16[16,32,2048]{2,1,0:T(8,128)(2,1)} %bitcast.90), calls=%async_computation.1 | async-start | bytes 4194304 | tf_op jit(solution)/shard_map/all_to_all | solution.py:68
  151.2 0.8 convolution_bitcast_fusion
  152.0 4.7 %convert_bitcast_fusion = bf16[1,2048,1024]{2,1,0:T(8,128)(2,1)} fusion(bf16[1,256,1024]{2,1,0:T(8,128)(2,1)S(1)} %copy-done.4, f32[256]{0:T(256)S(1)} %select_convert_fusion.1, bf16[256,2048]{1,0:T(8,128)(2,1)} %gather_fusion.3, pred[256]{0:T(512)(128)(4,1)S(1)} %compare_and_fusion), kind=kOutput, calls=%fused_computation.11 | convolution fusion | flops 1077149696 | bytes 5768448 | tf_op jit(solution)/shard_map/dot_general | solution.py:55
  156.7 33.4 %all-to-all-done.1 = bf16[16,32,2048]{2,1,0:T(8,128)(2,1)S(1)} async-done(((bf16[16,32,2048]{2,1,0:T(8,128)(2,1)}), bf16[16,32,2048]{2,1,0:T(8,128)(2,1)S(1)}, u32[]{:S(2)}, u32[]{:S(2)}) %all-to-all-start.1) | async-done | bytes 2097184 | tf_op jit(solution)/shard_map/all_to_all | solution.py:68
  190.1 0.5 fusion.28
  190.6 1.1 fusion.7
  191.7 40.6 %reduce-scatter.2.cloned.1.call-done = f32[128,16]{0,1:T(8,128)} async-done(((f32[2048,16]{0,1:T(8,128)}), f32[128,16]{0,1:T(8,128)}) %reduce-scatter.2.cloned.1.call-update) | async-done | bytes 8208 | tf_op jit(solution)/shard_map/reduce_scatter | solution.py:84
  (55 shorter events, 2.7 us)
Async XLA Ops:
  7.2 48.2 %copy-start = (bf16[128,2048]{1,0:T(8,128)(2,1)S(1)}, bf16[128,2048]{1,0:T(8,128)(2,1)}, u32[]{:S(2)}) copy-start(bf16[128,2048]{1,0:T(8,128)(2,1)} %param.6) | copy-start | bytes 1572868
  59.4 3.9 %copy-start.3 = (s32[1,256]{1,0:T(1,128)S(1)}, s32[1,256]{1,0:T(1,128)}, u32[]{:S(2)}) copy-start(s32[1,256]{1,0:T(1,128)} %param.10) | copy-start | bytes 3076
  59.5 4.3 %copy-start.1 = (f32[128,16]{0,1:T(8,128)S(1)}, f32[128,16]{0,1:T(8,128)}, u32[]{:S(2)}) copy-start(f32[128,16]{0,1:T(8,128)} %param.7) | copy-start | bytes 24580
  59.5 42.5 %all-to-all-start.2 = ((bf16[16,32,2048]{2,1,0:T(8,128)(2,1)}), bf16[16,32,2048]{2,1,0:T(8,128)(2,1)S(1)}, u32[]{:S(2)}, u32[]{:S(2)}) async-start(bf16[16,32,2048]{2,1,0:T(8,128)(2,1)} %select_select_fusion), calls=%async_computation.2 | async-start | bytes 4194304 | tf_op jit(solution)/shard_map/all_to_all | solution.py:44
  102.0 2.3 copy-start.4
  111.1 14.7 %all-to-all-start.3 = ((bf16[16,1,32]{2,1,0:T(2,128)(2,1)}), bf16[16,1,32]{2,1,0:T(2,128)(2,1)S(1)}, u32[]{:S(2)}, u32[]{:S(2)}) async-start(bf16[16,1,32]{2,1,0:T(2,128)(2,1)} %all_to_all.27), calls=%async_computation.3 | async-start | bytes 16384 | tf_op jit(solution)/shard_map/all_to_all | solution.py:69
  147.1 43.0 %all-to-all-start.1 = ((bf16[16,32,2048]{2,1,0:T(8,128)(2,1)}), bf16[16,32,2048]{2,1,0:T(8,128)(2,1)S(1)}, u32[]{:S(2)}, u32[]{:S(2)}) async-start(bf16[16,32,2048]{2,1,0:T(8,128)(2,1)} %bitcast.90), calls=%async_computation.1 | async-start | bytes 4194304 | tf_op jit(solution)/shard_map/all_to_all | solution.py:68
  150.8 81.5 %reduce-scatter.2.cloned.1.call-start = ((), (), s32[]{:S(2)}) async-start(), calls=%async_computation.5 | async-start | bytes 139264 | tf_op jit(solution)/shard_map/reduce_scatter | solution.py:84
  156.7 33.9 %copy-start.2 = (bf16[2048,16]{0,1:T(8,128)(2,1)S(1)}, bf16[2048,16]{0,1:T(8,128)(2,1)}, u32[]{:S(2)}) copy-start(bf16[2048,16]{0,1:T(8,128)(2,1)} %param.9) | copy-start | bytes 196612
Sparse Core Ops, SparseCore 0:
  154.5 77.7 reduce-scatter.1
where the time goes:
time: 240 us; the launch traced here: 239 us
  waiting for transfers between devices  119 us (50%)
  blocking collectives  52.6 us (22%)
  local copies, waits for them, and re-layouts  20.3 us (8%)
  starting transfers between devices  15.1 us (6%)
  matrix products  15.1 us (6%)
  between operations  14.3 us (6%)
  other arithmetic  2.66 us (1%)
    all_gather x1, blocking collectives, local(): all_lists = lax.all_gather(expert_picks, 'expert', axis=0, tiled=True)  42.8 us
    reduce_scatter x1, waiting for transfers between devices, local(): lax.psum_scatter(lax.dot_general(tokens, logit_grad, (((0,), (0,)), ((),...  40.6 us
    all_to_all x1, waiting for transfers between devices, local(): lax.all_to_all(send_rows, 'expert', split_axis=0, concat_axis=0, tiled=True)  38 us
    all_to_all x1, waiting for transfers between devices, local(): lax.all_to_all(back_rows, 'expert', split_axis=0, concat_axis=0, tiled=True)  33.4 us
    all_to_all x1, blocking collectives, local(): lax.all_to_all(send_gate, 'expert', split_axis=0, concat_axis=0, tiled=True)  9.85 us
    all_to_all x1, starting transfers between devices, local(): lax.all_to_all(back_gate, 'expert', split_axis=0, concat_axis=0, tiled=True)  7.45 us
    all_to_all x1, waiting for transfers between devices, local(): lax.all_to_all(back_gate, 'expert', split_axis=0, concat_axis=0, tiled=True)  7.18 us
  transfers between devices with their start and end apart: 4, of which 4 were waited for; matrix products, arithmetic and copies ran while one was open for 3% of the time, Pallas kernels for 0%

commit v1 on v0

v1 whole, which is shorter than its diff:
```python
import functools
import math

import jax
import jax.numpy as jnp
from jax import lax
from jax.experimental import pallas as pl
from jax.experimental.pallas import tpu as pltpu
from jax.sharding import PartitionSpec as P

F32 = jnp.float32
BF16 = jnp.bfloat16
MESH = pl.DeviceIdType.MESH


def remote(src, dst, send, recv, peer):
    return pltpu.make_async_remote_copy(
        src_ref=src, dst_ref=dst, send_sem=send, recv_sem=recv,
        device_id={"expert": peer}, device_id_type=MESH)


def loop(low, high, body):
    def step(i, carry):
        body(i)
        return carry
    lax.fori_loop(low, high, step, 0)


def kernel(n, nz, most,
           tokens, logits_t, weights, router_t, cols, picks_row, placed_row, cot,
           token_grad, weight_grad, router_grad,
           wbuf, wgbuf, probs, info_src, info_dst, sel, sel_t, scaled, rg,
           tokbuf, fwd_src, rowbuf, bwd_src, bwdbuf, zin, zsend,
           score_src, score_dst, rs_src, rs_dst,
           w_sem, wg_sem, i_send, i_recv, a_send, a_recv, f_send, f_recv,
           b_send, b_recv, z_send, z_recv, s_send, s_recv, r_send, r_recv):
    plane = n // nz
    tok, width = tokens.shape
    hidden = cot.shape[1]
    cap = cot.shape[0]
    me = lax.axis_index("expert")
    z = me // plane
    c = me % plane

    w_copy = pltpu.make_async_copy(weights.at[0], wbuf, w_sem)
    w_copy.start()
    barrier = pltpu.get_barrier_semaphore()
    loop(1, n, lambda i: pl.semaphore_signal(
        barrier, inc=1, device_id={"expert": lax.rem(me + i, n)}, device_id_type=MESH))

    scores = logits_t[...]
    exps = jnp.exp(scores - jnp.max(scores, axis=0, keepdims=True))
    probs[...] = exps / jnp.sum(exps, axis=0, keepdims=True)
    info_src[...] = jnp.zeros_like(info_src)

    def fill_info(e):
        info_src[e, 0:1, :] = probs[pl.ds(e, 1), :]
        for k in range(cap // 128):
            info_src[e, 1 + k:2 + k, :] = picks_row[:, k * 128:(k + 1) * 128]
    loop(0, n, fill_info)
    info_dst[me] = info_src[me]
    pl.semaphore_wait(barrier, n - 1)

    def info_copy(peer):
        return remote(info_src.at[peer], info_dst.at[me], i_send.at[peer], i_recv.at[me], peer)

    def info_arrival(peer):
        return remote(info_src.at[peer], info_dst.at[peer], i_send.at[peer], i_recv.at[peer], peer)

    loop(1, n, lambda i: info_copy(lax.rem(me + i, n)).start())

    def up_own():
        return remote(tokens, tokbuf.at[z], a_send.at[0, z], a_recv.at[z], me + plane)

    def down_own():
        return remote(tokens, tokbuf.at[z], a_send.at[1, z], a_recv.at[z], me - plane)

    def up_pass(src):
        return remote(tokbuf.at[src], tokbuf.at[src], a_send.at[0, src], a_recv.at[src], me + plane)

    def down_pass(src):
        return remote(tokbuf.at[src], tokbuf.at[src], a_send.at[1, src], a_recv.at[src], me - plane)

    @pl.when(z < nz - 1)
    def _():
        up_own().start()

    @pl.when(z > 0)
    def _():
        down_own().start()

    loop(1, n, lambda i: info_arrival(lax.rem(me + i, n)).wait_recv())

    tok_col = lax.broadcasted_iota(jnp.int32, (tok, 128), 0).astype(F32)
    slot_lane = lax.broadcasted_iota(jnp.int32, (tok, plane * most), 1).astype(F32)

    def build_sel(zs):
        base = ((zs * plane + c) * tok).astype(F32)

        def one(e, acc):
            rank = jnp.zeros((tok, 128), F32)
            member = jnp.zeros((tok, 128), F32)
            for k in range(cap // 128):
                rel = info_dst[z * plane + e, 1 + k:2 + k, :] - base
                rank += jnp.where((rel >= 0.0) & (rel < tok_col), 1.0, 0.0)
                member += jnp.where(rel == tok_col, 1.0, 0.0)
            rank = jnp.sum(rank, axis=1, keepdims=True)
            member = jnp.sum(member, axis=1, keepdims=True)
            first = (e * most).astype(F32)
            return acc + jnp.where(slot_lane == rank + first, member, 0.0)

        made = lax.fori_loop(0, plane, one, jnp.zeros((tok, plane * most), F32))
        sel_t[zs] = made.astype(BF16)
        sel[zs] = made.T.astype(BF16)
    loop(0, nz, build_sel)

    def fwd_copy(zs, c2):
        return remote(fwd_src.at[zs, pl.ds(pl.multiple_of(c2 * most, most), most), :],
                      rowbuf.at[pl.ds(pl.multiple_of((zs * plane + c) * most, most), most), :],
                      f_send.at[zs, c2], f_recv.at[zs, c], z * plane + c2)

    def fwd_arrival(zs, c2):
        return remote(fwd_src.at[zs, pl.ds(pl.multiple_of(c2 * most, most), most), :],
                      rowbuf.at[pl.ds(pl.multiple_of((zs * plane + c2) * most, most), most), :],
                      f_send.at[zs, c2], f_recv.at[zs, c2], z * plane + c2)

    def forward(zs, block):
        tile = 512

        def piece(t):
            lanes = pl.ds(pl.multiple_of(t * tile, tile), tile)
            fwd_src[zs, :, lanes] = jnp.dot(
                sel[zs], block[:, lanes], preferred_element_type=F32).astype(BF16)
        loop(0, width // tile, piece)
        loop(1, plane, lambda i: fwd_copy(zs, lax.rem(c + i, plane)).start())
        rowbuf[pl.ds(pl.multiple_of((zs * plane + c) * most, most), most), :] = (
            fwd_src[zs, pl.ds(pl.multiple_of(c * most, most), most), :])

    forward(z, tokens)

    picks_col = cols[:, 0:1]
    placed_col = cols[:, 1:2]
    lane = lax.broadcasted_iota(jnp.int32, (cap, 128), 1).astype(F32)

    def add_gate(o, acc):
        hit = (picks_col - (o * tok).astype(F32)) == lane
        return acc + jnp.where(hit, info_dst[o, 0:1, :], 0.0)
    gate = jnp.sum(lax.fori_loop(0, n, add_gate, jnp.zeros((cap, 128), F32)), axis=1, keepdims=True)
    gate = gate.astype(BF16).astype(F32)
    scaled[...] = (gate * cot[...].astype(F32)).astype(BF16)
    w_copy.wait()

    def row_tile(t):
        lanes = pl.ds(pl.multiple_of(t * 256, 256), 256)
        rg[:, lanes] = lax.dot_general(
            scaled[...], wbuf[lanes, :], (((1,), (1,)), ((), ())),
            preferred_element_type=F32).astype(BF16)
    loop(0, width // 256, row_tile)

    def bwd_copy(zd, c2):
        return remote(bwd_src.at[zd, pl.ds(pl.multiple_of(c2 * most, most), most), :],
                      bwdbuf.at[zd, pl.ds(pl.multiple_of(c * most, most), most), :],
                      b_send.at[zd, c2], b_recv.at[zd, c], z * plane + c2)

    def bwd_arrival(zd, c2):
        return remote(bwd_src.at[zd, pl.ds(pl.multiple_of(c2 * most, most), most), :],
                      bwdbuf.at[zd, pl.ds(pl.multiple_of(c2 * most, most), most), :],
                      b_send.at[zd, c2], b_recv.at[zd, c2], z * plane + c2)

    slot_row = lax.broadcasted_iota(jnp.int32, (plane * most, cap), 0).astype(F32)

    def backward(zd):
        low = (zd * plane * most).astype(F32)
        spread = jnp.where(slot_row == placed_row[...] - low, 1.0, 0.0).astype(BF16)

        def piece(t):
            lanes = pl.ds(pl.multiple_of(t * 512, 512), 512)
            bwd_src[zd, :, lanes] = jnp.dot(
                spread, rg[:, lanes], preferred_element_type=F32).astype(BF16)
        loop(0, width // 512, piece)
        loop(1, plane, lambda i: bwd_copy(zd, lax.rem(c + i, plane)).start())
        mine = pl.ds(pl.multiple_of(c * most, most), most)
        bwdbuf[zd, mine, :] = bwd_src[zd, mine, :]

    for far in range(nz - 1, 0, -1):
        @pl.when(z + far < nz)
        def _(far=far):
            backward(z + far)

        @pl.when(z - far >= 0)
        def _(far=far):
            backward(z - far)
    backward(z)

    def chain(dest, slot, has_in, out_slot, peer):
        copy = remote(zsend.at[dest], zin.at[out_slot], z_send.at[dest], z_recv.at[out_slot], peer)
        loop(1, plane, lambda i: bwd_arrival(dest, lax.rem(c + i, plane)).wait_recv())

        @pl.when(has_in)
        def _():
            remote(zsend.at[dest], zin.at[slot], z_send.at[dest], z_recv.at[slot], peer).wait_recv()

            def piece(t):
                lanes = pl.ds(pl.multiple_of(t * 512, 512), 512)
                zsend[dest, :, lanes] = (jnp.dot(
                    sel_t[dest], bwdbuf[dest, :, lanes], preferred_element_type=F32)
                    + zin[slot, :, lanes].astype(F32)).astype(BF16)
            loop(0, width // 512, piece)

        @pl.when(jnp.logical_not(has_in))
        def _():
            def piece(t):
                lanes = pl.ds(pl.multiple_of(t * 512, 512), 512)
                zsend[dest, :, lanes] = jnp.dot(
                    sel_t[dest], bwdbuf[dest, :, lanes], preferred_element_type=F32).astype(BF16)
            loop(0, width // 512, piece)
        copy.start()

    for step in range(nz):
        if step > 0:
            @pl.when(z - step >= 0)
            def _(step=step):
                src = z - step
                up_pass(src).wait_recv()

                @pl.when(z < nz - 1)
                def _():
                    up_pass(src).start()
                forward(src, tokbuf.at[src])

            @pl.when(z + step < nz)
            def _(step=step):
                src = z + step
                down_pass(src).wait_recv()

                @pl.when(z > 0)
                def _():
                    down_pass(src).start()
                forward(src, tokbuf.at[src])

        up_dest = nz - 1 - (step - z)

        @pl.when((step >= z) & (up_dest > z))
        def _(up_dest=up_dest):
            chain(up_dest, up_dest, z > 0, up_dest, me + plane)

        down_dest = step - (nz - 1 - z)

        @pl.when((down_dest >= 0) & (down_dest < z))
        def _(down_dest=down_dest):
            chain(down_dest, down_dest, z < nz - 1,
                  jnp.where(down_dest == z - 1, nz, down_dest), me - plane)

    def rows_arrived(k):
        zs = k // plane
        c2 = k % plane

        @pl.when(c2 != c)
        def _():
            fwd_arrival(zs, c2).wait_recv()
    loop(0, n, rows_arrived)
    slot_lanes = lax.broadcasted_iota(jnp.int32, (cap, n * most), 1).astype(F32)
    compact = jnp.where(slot_lanes == placed_col, 1.0, 0.0).astype(BF16)

    rc = rg

    def compact_tile(t):
        lanes = pl.ds(pl.multiple_of(t * 256, 256), 256)
        rc[:, lanes] = jnp.dot(compact, rowbuf[:, lanes], preferred_element_type=F32).astype(BF16)
    loop(0, width // 256, compact_tile)

    def active_tile(t, acc):
        lanes = pl.ds(pl.multiple_of(t * 256, 256), 256)
        active = jnp.dot(rc[...], wbuf[:, lanes], preferred_element_type=F32)
        return acc + jnp.sum(cot[:, lanes].astype(F32) * active, axis=1, keepdims=True)
    gate_grad = lax.fori_loop(0, hidden // 256, active_tile, jnp.zeros((cap, 1), F32))
    gate_grad = gate_grad.astype(BF16).astype(F32)

    def score_copy(peer):
        return remote(score_src.at[peer], score_dst.at[me], s_send.at[peer], s_recv.at[me], peer)

    def score_arrival(peer):
        return remote(score_src.at[peer], score_dst.at[peer], s_send.at[peer], s_recv.at[peer], peer)

    score_src[...] = jnp.zeros_like(score_src)

    def score_row(i):
        o = lax.rem(me + i, n)
        hit = (picks_col - (o * tok).astype(F32)) == lane
        score_src[o, 0:1, :] = jnp.sum(jnp.where(hit, gate_grad, 0.0), axis=0, keepdims=True)

    def score_send(i):
        score_row(i)
        score_copy(lax.rem(me + i, n)).start()
    loop(1, n, score_send)
    score_row(0)
    score_dst[me] = score_src[me]

    def weight_tile(t):
        lanes = pl.ds(pl.multiple_of(t * 256, 256), 256)
        wgbuf[lanes, :] = lax.dot_general(
            rc[:, lanes], scaled[...], (((0,), (0,)), ((), ())),
            preferred_element_type=F32).astype(BF16)
    loop(0, width // 256, weight_tile)
    wg_copy = pltpu.make_async_copy(wgbuf, weight_grad.at[0], wg_sem)
    wg_copy.start()

    loop(1, n, lambda i: score_arrival(lax.rem(me + i, n)).wait_recv())
    score = score_dst[:, 0, :]
    prob = probs[...]
    inner = jnp.sum(prob * score, axis=0, keepdims=True)
    logit_grad = prob * (score - inner)
    logit_col = logit_grad.T.astype(BF16)
    logit_grad = logit_grad.astype(BF16)
    share = width // n
    wide = share % 128 == 0

    def router_tile(t):
        lanes = pl.ds(pl.multiple_of(t * 512, 512), 512)
        part = jnp.dot(logit_grad, tokens[:, lanes], preferred_element_type=F32)
        if wide:
            rs_src[:, lanes] = part
        else:
            rs_src[lanes, :] = part.T
    loop(0, width // 512, router_tile)

    def share_of(d):
        if wide:
            return rs_src.at[:, pl.ds(pl.multiple_of(d * share, share), share)]
        return rs_src.at[pl.ds(pl.multiple_of(d * share, share), share), :]

    def rs_copy(peer):
        return remote(share_of(peer), rs_dst.at[me], r_send.at[peer], r_recv.at[me], peer)

    def rs_arrival(peer):
        return remote(share_of(peer), rs_dst.at[peer], r_send.at[peer], r_recv.at[peer], peer)
    loop(1, n, lambda i: rs_copy(lax.rem(me + i, n)).start())
    rs_dst[me] = share_of(me)[...]

    loop(1, plane, lambda i: bwd_arrival(z, lax.rem(c + i, plane)).wait_recv())

    @pl.when(z == 0)
    def _():
        zin[z] = jnp.zeros(zin.shape[1:], BF16)

    @pl.when(z == nz - 1)
    def _():
        zin[nz] = jnp.zeros(zin.shape[1:], BF16)

    @pl.when(z > 0)
    def _():
        remote(zsend.at[z], zin.at[z], z_send.at[z], z_recv.at[z], me).wait_recv()

    @pl.when(z < nz - 1)
    def _():
        remote(zsend.at[z], zin.at[nz], z_send.at[z], z_recv.at[nz], me).wait_recv()

    def final_tile(t):
        lanes = pl.ds(pl.multiple_of(t * 512, 512), 512)
        total = jnp.dot(sel_t[z], bwdbuf[z, :, lanes], preferred_element_type=F32)
        total += zin[z, :, lanes].astype(F32) + zin[nz, :, lanes].astype(F32)
        total += jnp.dot(logit_col, router_t[:, lanes], preferred_element_type=F32)
        token_grad[:, lanes] = total.astype(BF16)
    loop(0, width // 512, final_tile)

    loop(1, n, lambda i: rs_arrival(lax.rem(me + i, n)).wait_recv())
    total = jnp.sum(rs_dst[...], axis=0)
    router_grad[...] = total.T if wide else total

    def sent(i):
        peer = lax.rem(me + i, n)
        info_copy(peer).wait_send()
        score_copy(peer).wait_send()
        rs_copy(peer).wait_send()
    loop(1, n, sent)

    def sent_plane(k):
        zs = k // plane
        c2 = k % plane

        @pl.when(c2 != c)
        def _():
            fwd_copy(zs, c2).wait_send()
            bwd_copy(zs, c2).wait_send()
    loop(0, n, sent_plane)

    def sent_z(zs):
        @pl.when((z < nz - 1) & (zs <= z))
        def _():
            up_pass(zs).wait_send()

        @pl.when((z > 0) & (zs >= z))
        def _():
            down_pass(zs).wait_send()

        @pl.when(zs != z)
        def _():
            remote(zsend.at[zs], zin.at[zs], z_send.at[zs], z_recv.at[zs], me).wait_send()
    loop(0, nz, sent_z)
    wg_copy.wait()


def local(tokens, logits, weights, router_weight, expert_picks, cotangent):
    n = lax.axis_size("expert")
    nz = 2 ** math.ceil(math.log2(n) / 3)
    plane = n // nz
    tok, width = tokens.shape
    cap = expert_picks.shape[1]
    hidden = weights.shape[2]
    slots = 2 * cap // n
    most = max(slots, 16)
    wanted = expert_picks[0]
    owner = wanted // tok
    before = jnp.sum((wanted[None, :] < (owner * tok)[:, None]).astype(jnp.int32), axis=1)
    placed = (owner * most + jnp.arange(cap, dtype=jnp.int32) - before).astype(F32)
    picks = wanted.astype(F32)
    cols = jnp.stack([picks, placed], axis=1)
    share = width // n
    rs_block = (n, share) if share % 128 == 0 else (share, n)
    rs_full = (n, width) if share % 128 == 0 else (width, n)
    vmem = pl.BlockSpec(memory_space=pltpu.VMEM)
    hbm = pl.BlockSpec(memory_space=pl.ANY)
    dma = pltpu.SemaphoreType.DMA
    flops = 2 * cap * width * hidden * 3
    return pl.pallas_call(
        functools.partial(kernel, n, nz, most),
        out_shape=(
            jax.ShapeDtypeStruct((tok, width), BF16),
            jax.ShapeDtypeStruct((1, width, hidden), BF16),
            jax.ShapeDtypeStruct((share, n), F32),
        ),
        in_specs=[vmem, vmem, hbm, vmem, vmem, vmem, vmem, vmem],
        out_specs=(vmem, hbm, vmem),
        scratch_shapes=[
            pltpu.VMEM((width, hidden), BF16),
            pltpu.VMEM((width, hidden), BF16),
            pltpu.VMEM((n, tok), F32),
            pltpu.VMEM((n, 8, 128), F32),
            pltpu.VMEM((n, 8, 128), F32),
            pltpu.VMEM((nz, plane * most, tok), BF16),
            pltpu.VMEM((nz, tok, plane * most), BF16),
            pltpu.VMEM((cap, hidden), BF16),
            pltpu.VMEM((cap, width), BF16),
            pltpu.VMEM((nz, tok, width), BF16),
            pltpu.VMEM((nz, plane * most, width), BF16),
            pltpu.VMEM((n * most, width), BF16),
            pltpu.VMEM((nz, plane * most, width), BF16),
            pltpu.VMEM((nz, plane * most, width), BF16),
            pltpu.VMEM((nz + 1, tok, width), BF16),
            pltpu.VMEM((nz, tok, width), BF16),
            pltpu.VMEM((n, 8, 128), F32),
            pltpu.VMEM((n, 8, 128), F32),
            pltpu.VMEM(rs_full, F32),
            pltpu.VMEM((n,) + rs_block, F32),
            dma, dma,
            dma((n,)), dma((n,)),
            dma((2, nz)), dma((nz,)),
            dma((nz, plane)), dma((nz, plane)),
            dma((nz, plane)), dma((nz, plane)),
            dma((nz,)), dma((nz + 1,)),
            dma((n,)), dma((n,)),
            dma((n,)), dma((n,)),
        ],
        compiler_params=pltpu.CompilerParams(
            collective_id=0, has_side_effects=True, vmem_limit_bytes=62 * 1024 * 1024),
        cost_estimate=pl.CostEstimate(flops=flops, bytes_accessed=12 * 2 ** 20, transcendentals=0),
    )(tokens, logits.T, weights, router_weight.T, cols, picks[None, :], placed[None, :], cotangent[0])


def solution(mesh):
    in_specs = (
        P(("dp", "expert"), None),
        P(("dp", "expert"), None),
        P("expert", None, None),
        P(),
        P(("dp", "expert"), None),
        P(("dp", "expert"), None, None),
    )
    out_specs = (
        P(("dp", "expert"), None),
        P(("dp", "expert"), None, None),
        P(("dp", "expert"), None),
    )
    return jax.shard_map(local, mesh=mesh, in_specs=in_specs, out_specs=out_specs, check_vma=False)
```

time: 240 us -> 94 us (0.39)
  waiting for transfers between devices: 119 us -> 0 us
  Pallas kernels: 0 us -> 80.6 us
  blocking collectives: 52.6 us -> 0 us
  matrix products: 15.1 us -> 0 us
  starting transfers between devices: 15.1 us -> 0 us
  between operations: 14.3 us -> 0.64 us
  local copies, waits for them, and re-layouts: 20.3 us -> 8.83 us
    pallas_call x0 -> x1, Pallas kernels: none -> 80.6 us  [local(): pl.pallas_call(functools.partial(kernel, n, nz, most), out_shape=(jax.Sha...]
    all_to_all x3 -> x0, waiting for transfers between devices: 78.6 us -> none  [the longest x1 38 us: local(): lax.all_to_all(send_rows, 'expert', split_axis=0, concat_axis=0, tiled=True)]
    all_gather x1 -> x0, blocking collectives: 42.8 us -> none  [local(): all_lists = lax.all_gather(expert_picks, 'expert', axis=0, tiled=True)]
    reduce_scatter x1 -> x0, waiting for transfers between devices: 40.6 us -> none  [local(): lax.psum_scatter(lax.dot_general(tokens, logit_grad, (((0,), (0,)), ((),...]
    dot_general x8 -> x0, matrix products: 15.1 us -> none  [the longest x1 4.67 us: local(): lax.dot_general(picked_rows, scaled, (((0,), (0,)), ((), ())), preferred_...]
    all_to_all x3 -> x0, starting transfers between devices: 15 us -> none  [the longest x1 7.45 us: local(): lax.all_to_all(back_gate, 'expert', split_axis=0, concat_axis=0, tiled=True)]
    gather x7 -> x0, local copies, waits for them, and re-layouts: 12.8 us -> none  [the longest x3 4.67 us: local(): located = jnp.take_along_axis(all_lists, positions, axis=1) - slice_low]
    all_to_all x1 -> x0, blocking collectives: 9.85 us -> none  [local(): lax.all_to_all(send_gate, 'expert', split_axis=0, concat_axis=0, tiled=True)]
  transfers between devices with their start and end apart: 4 -> 0, of which waited for: 4 -> 0; matrix products, arithmetic and copies ran while one was open for 3% -> 0% of each run, Pallas kernels for 0% -> 0%
where the time goes in v1:
time: 94 us; the launch traced here: 93.6 us
  Pallas kernels  80.6 us (86%)
  local copies, waits for them, and re-layouts  8.83 us (9%)
  other arithmetic  3.58 us (4%)
    pallas_call x1, Pallas kernels, local(): pl.pallas_call(functools.partial(kernel, n, nz, most), out_shape=(jax.Sha...  80.6 us
    unnamed x2, local copies, waits for them, and re-layouts  6.52 us
    convert_element_type x2, other arithmetic, local(): (owner * most + jnp.arange(cap, dtype=jnp.int32) - before).astype(F32)  2.03 us

profile of v1, /device:TPU:0, one launch (start us, length us, event | category | flops | bytes accessed | tf_op | source)
XLA Modules:
  0.0 93.6 jit_solution(17483766530211833257)
XLA Ops:
  0.6 0.7 fusion
  1.3 0.9 convert_reduce_fusion
  2.2 0.7 subtract_convert_fusion.1
  2.9 1.3 %subtract_convert_fusion = (f32[1,256]{1,0:T(1,128)}, f32[1,256]{1,0:T(1,128)}, f32[256,1]{0,1:T(1,128)S(1)}) fusion(s32[1,256]{1,0:T(1,128)S(1)} %bitcast.20, s32[1,256]{1,0:T(1,128)} %param.10), kind=kLoop, calls=%fused_computation.16 | loop fusion | flops 5376 | bytes 5120 | tf_op jit(solution)/shard_map/convert_element_type | solution.py:415
  4.2 0.8 copy.19.cols
  5.0 80.6 %shard_map.85 = (bf16[128,2048]{1,0:T(8,128)(2,1)}, bf16[1,2048,1024]{2,1,0:T(8,128)(2,1)}, f32[128,16]{1,0:T(8,128)}) custom-call(bf16[128,2048]{1,0:T(8,128)(2,1)} %tokens.1, f32[16,128]{1,0:T(8,128)} %bitcast.23, bf16[1,2048,1024]{2,1,0:T(8,128)(2,1)} %weights.1, bf16[16,2048]{1,0:T(8,128)(2,1)} %bitcast.22, f32[256,2]{1,0:T(8,128)} %copy.19.cols, ...), custom_call_target="tpu_custom_call" | custom-call | flops 3221225472 | bytes 12582912 | tf_op jit(solution)/shard_map/pallas_call | solution.py:425
  85.6 1.5 %copy.20 = f32[128,16]{0,1:T(8,128)} copy(f32[128,16]{1,0:T(8,128)} %get-tuple-element.14) | data formatting | bytes 16384 | tf_op jit(solution)/shard_map/pallas_call | solution.py:425
  87.1 1.9 %copy.23 = bf16[128,2048]{1,0:T(8,128)(2,1)} copy(bf16[128,2048]{1,0:T(8,128)(2,1)} %get-tuple-element.21) | data formatting | bytes 1048576
  89.0 4.6 %copy.24 = bf16[1,2048,1024]{2,1,0:T(8,128)(2,1)} copy(bf16[1,2048,1024]{2,1,0:T(8,128)(2,1)} %get-tuple-element.22) | data formatting | bytes 8388608
  (1 shorter events, 0.0 us)

commit v2 on v1

v2 whole, which is shorter than its diff:
```python
import functools
import math

import jax
import jax.numpy as jnp
from jax import lax
from jax.experimental import pallas as pl
from jax.experimental.pallas import tpu as pltpu
from jax.sharding import PartitionSpec as P

F32 = jnp.float32
BF16 = jnp.bfloat16
MESH = pl.DeviceIdType.MESH
PARTS = 2


def remote(src, dst, send, recv, peer):
    return pltpu.make_async_remote_copy(
        src_ref=src, dst_ref=dst, send_sem=send, recv_sem=recv,
        device_id={"expert": peer}, device_id_type=MESH)


def loop(low, high, body):
    def step(i, carry):
        body(i)
        return carry
    lax.fori_loop(low, high, step, 0)


def kernel(n, nz, most, parts,
           tokens, logits_t, weights, router_t, picks_ref, cot,
           token_grad, rows_out, scaled_out, router_grad,
           wbuf, probs, info_src, info_dst, sel, sel_t, scaled, rg,
           tokbuf, fwd_src, rowbuf, bwd_src, bwdbuf, zin, zsend,
           score_src, score_dst, rs_src, rs_dst,
           w_sem, out_sem, i_send, i_recv, a_send, a_recv, f_send, f_recv,
           b_send, b_recv, z_send, z_recv, s_send, s_recv, r_send, r_recv):
    plane = n // nz
    tok, width = tokens.shape
    piece = width // parts
    tile = min(512, piece)
    hidden = cot.shape[1]
    cap = cot.shape[0]
    me = lax.axis_index("expert")
    z = me // plane
    c = me % plane
    group = plane * most

    w_copy = pltpu.make_async_copy(weights.at[0], wbuf, w_sem)
    w_copy.start()
    barrier = pltpu.get_barrier_semaphore()
    loop(1, n, lambda i: pl.semaphore_signal(
        barrier, inc=1, device_id={"expert": lax.rem(me + i, n)}, device_id_type=MESH))

    scores = logits_t[...]
    exps = jnp.exp(scores - jnp.max(scores, axis=0, keepdims=True))
    probs[...] = exps / jnp.sum(exps, axis=0, keepdims=True)
    picks_row = picks_ref[...].astype(F32)
    info_src[...] = jnp.zeros_like(info_src)

    def fill_info(e):
        info_src[e, 0:1, :] = probs[pl.ds(e, 1), :]
        for k in range(cap // 128):
            info_src[e, 1 + k:2 + k, :] = picks_row[:, k * 128:(k + 1) * 128]
    loop(0, n, fill_info)
    info_dst[me] = info_src[me]
    for h in range(parts):
        tokbuf[z, h] = tokens[:, h * piece:(h + 1) * piece]

    picks_wide = jnp.concatenate(
        [jnp.broadcast_to(picks_row[:, k * 128:(k + 1) * 128], (128, 128)).T
         for k in range(cap // 128)], axis=0)
    picks_col = picks_wide[:, 0:1]

    def padded(values, other, axis, order):
        owner = jnp.floor(values * (1.0 / tok))
        before = jnp.sum(jnp.where(other < owner * tok, 1.0, 0.0), axis=axis, keepdims=True)
        return owner * most + order.astype(F32) - before
    placed_col = padded(picks_col, picks_row, 1, lax.broadcasted_iota(jnp.int32, (cap, 1), 0))
    placed_row = padded(picks_row, picks_col, 0, lax.broadcasted_iota(jnp.int32, (1, cap), 1))
    pl.semaphore_wait(barrier, n - 1)

    def info_copy(peer):
        return remote(info_src.at[peer], info_dst.at[me], i_send.at[peer], i_recv.at[me], peer)

    def info_arrival(peer):
        return remote(info_src.at[peer], info_dst.at[peer], i_send.at[peer], i_recv.at[peer], peer)

    loop(1, n, lambda i: info_copy(lax.rem(me + i, n)).start())

    def next_of(way):
        return me + plane * (1 - 2 * way)

    def goes_on(way):
        return jnp.where(way == 0, z < nz - 1, z > 0)

    def token_copy(way, src, h):
        return remote(tokbuf.at[src, h], tokbuf.at[src, h],
                      a_send.at[way, src, h], a_recv.at[src, h], next_of(way))

    def token_start(k):
        way, h = k % 2, k // 2

        @pl.when(goes_on(way))
        def _():
            token_copy(way, z, h).start()
    loop(0, 2 * parts, token_start)
    loop(1, n, lambda i: info_arrival(lax.rem(me + i, n)).wait_recv())

    lane = lax.broadcasted_iota(jnp.int32, (cap, 128), 1).astype(F32)

    def add_gate(o, acc):
        hit = (picks_col - (o * tok).astype(F32)) == lane
        return acc + jnp.where(hit, info_dst[o, 0:1, :], 0.0)
    gate = jnp.sum(lax.fori_loop(0, n, add_gate, jnp.zeros((cap, 128), F32)), axis=1, keepdims=True)
    gate = gate.astype(BF16).astype(F32)
    scaled[...] = (gate * cot[...].astype(F32)).astype(BF16)
    scaled_copy = pltpu.make_async_copy(scaled, scaled_out, out_sem.at[0])
    scaled_copy.start()
    w_copy.wait()

    def row_tile(t):
        rows = pl.ds(pl.multiple_of(t * tile, tile), tile)
        per = piece // tile
        lanes = pl.ds(pl.multiple_of((t % per) * tile, tile), tile)
        rg[t // per, :, lanes] = lax.dot_general(
            scaled[...], wbuf[rows, :], (((1,), (1,)), ((), ())),
            preferred_element_type=F32).astype(BF16)
    loop(0, width // tile, row_tile)

    def mine_of(c2):
        return pl.ds(pl.multiple_of(c2 * most, most), most)

    def bwd_copy(zd, h, c2):
        return remote(bwd_src.at[zd, h, mine_of(c2), :], bwdbuf.at[zd, h, mine_of(c), :],
                      b_send.at[zd, h, c2], b_recv.at[zd, h, c], z * plane + c2)

    def bwd_arrival(zd, h, c2):
        return remote(bwd_src.at[zd, h, mine_of(c2), :], bwdbuf.at[zd, h, mine_of(c2), :],
                      b_send.at[zd, h, c2], b_recv.at[zd, h, c2], z * plane + c2)

    slot_row = lax.broadcasted_iota(jnp.int32, (group, cap), 0).astype(F32)

    def backward(zd, h):
        low = (zd * group).astype(F32)
        spread = jnp.where(slot_row == placed_row - low, 1.0, 0.0).astype(BF16)
        for t in range(piece // tile):
            lanes = slice(t * tile, (t + 1) * tile)
            bwd_src[zd, h, :, lanes] = jnp.dot(
                spread, rg[h, :, lanes], preferred_element_type=F32).astype(BF16)
        loop(1, plane, lambda i: bwd_copy(zd, h, lax.rem(c + i, plane)).start())
        bwdbuf[zd, h, mine_of(c), :] = bwd_src[zd, h, mine_of(c), :]

    def chain_place(q, way):
        start = jnp.where(way == 0, z, nz - 1 - z)
        k = q - start
        block = jnp.maximum(k, 0) // parts
        dest = jnp.where(way == 0, nz - 1 - block, block)
        valid = (k >= 0) & (block < nz - 1 - start)
        return valid, jnp.minimum(jnp.maximum(dest, 0), nz - 1), jnp.maximum(k, 0) % parts, start > 0

    def backward_at(q):
        def one(way):
            valid, dest, h, _ = chain_place(q, way)

            @pl.when(valid)
            def _():
                backward(dest, h)
        loop(0, 2, one)

    ahead = parts
    loop(0, ahead, backward_at)

    tok_col = lax.broadcasted_iota(jnp.int32, (tok, 128), 0).astype(F32)
    slot_lane = lax.broadcasted_iota(jnp.int32, (tok, group), 1).astype(F32)

    def build_sel(zs):
        base = ((zs * plane + c) * tok).astype(F32)

        def one(e, acc):
            rank = jnp.zeros((tok, 128), F32)
            member = jnp.zeros((tok, 128), F32)
            for k in range(cap // 128):
                rel = info_dst[z * plane + e, 1 + k:2 + k, :] - base
                rank += jnp.where((rel >= 0.0) & (rel < tok_col), 1.0, 0.0)
                member += jnp.where(rel == tok_col, 1.0, 0.0)
            rank = jnp.sum(rank, axis=1, keepdims=True)
            member = jnp.sum(member, axis=1, keepdims=True)
            first = (e * most).astype(F32)
            return acc + jnp.where(slot_lane == rank + first, member, 0.0)

        made = lax.fori_loop(0, plane, one, jnp.zeros((tok, group), F32))
        sel_t[zs] = made.astype(BF16)
        sel[zs] = made.T.astype(BF16)
    loop(0, nz, build_sel)

    def rows_of(zs, c2):
        return pl.ds(pl.multiple_of((zs * plane + c2) * most, most), most)

    def fwd_copy(zs, h, c2):
        return remote(fwd_src.at[zs, h, mine_of(c2), :], rowbuf.at[h, rows_of(zs, c), :],
                      f_send.at[zs, h, c2], f_recv.at[zs, h, c], z * plane + c2)

    def fwd_arrival(zs, h, c2):
        return remote(fwd_src.at[zs, h, mine_of(c2), :], rowbuf.at[h, rows_of(zs, c2), :],
                      f_send.at[zs, h, c2], f_recv.at[zs, h, c2], z * plane + c2)

    def forward_at(q, way):
        far, h = q // parts, q % parts
        src = z + (2 * way - 1) * far

        @pl.when((src >= 0) & (src < nz) & ((far > 0) | (way == 0)))
        def _():
            @pl.when(far > 0)
            def _():
                token_copy(way, src, h).wait_recv()

                @pl.when(goes_on(way))
                def _():
                    token_copy(way, src, h).start()
            for t in range(piece // tile):
                lanes = slice(t * tile, (t + 1) * tile)
                fwd_src[src, h, :, lanes] = jnp.dot(
                    sel[src], tokbuf[src, h, :, lanes], preferred_element_type=F32).astype(BF16)
            loop(1, plane, lambda i: fwd_copy(src, h, lax.rem(c + i, plane)).start())
            rowbuf[h, rows_of(src, c), :] = fwd_src[src, h, mine_of(c), :]

    def chain_at(q, way):
        valid, dest, h, has_in = chain_place(q, way)
        out_slot = jnp.where((way == 1) & (dest == z - 1), nz, dest)

        @pl.when(valid)
        def _():
            loop(1, plane, lambda i: bwd_arrival(dest, h, lax.rem(c + i, plane)).wait_recv())

            @pl.when(has_in)
            def _():
                remote(zsend.at[dest, h], zin.at[dest, h], z_send.at[dest, h],
                       z_recv.at[dest, h], me).wait_recv()

            @pl.when(jnp.logical_not(has_in))
            def _():
                zin[dest, h] = jnp.zeros(zin.shape[2:], BF16)
            for t in range(piece // tile):
                lanes = slice(t * tile, (t + 1) * tile)
                zsend[dest, h, :, lanes] = (jnp.dot(
                    sel_t[dest], bwdbuf[dest, h, :, lanes], preferred_element_type=F32)
                    + zin[dest, h, :, lanes].astype(F32)).astype(BF16)
            remote(zsend.at[dest, h], zin.at[out_slot, h], z_send.at[dest, h],
                   z_recv.at[out_slot, h], next_of(way)).start()

    def substep(q):
        loop(0, 2, lambda way: forward_at(q, way))
        backward_at(q + ahead)

        @pl.when((q >= parts * (nz - 2)) & (q < parts * (nz - 1)))
        def _():
            backward(z, q % parts)
        loop(0, 2, lambda way: chain_at(q, way))
    loop(0, nz * parts, substep)

    slot_lanes = lax.broadcasted_iota(jnp.int32, (cap, n * most), 1).astype(F32)
    compact = jnp.where(slot_lanes == placed_col, 1.0, 0.0).astype(BF16)
    rc = rg

    def gate_part(h, total):
        def rows_arrived(k):
            zs = k // plane
            c2 = k % plane

            @pl.when(c2 != c)
            def _():
                fwd_arrival(zs, h, c2).wait_recv()
        loop(0, n, rows_arrived)
        for t in range(piece // tile):
            lanes = slice(t * tile, (t + 1) * tile)
            rc[h, :, lanes] = jnp.dot(
                compact, rowbuf[h, :, lanes], preferred_element_type=F32).astype(BF16)

        def active_tile(t, acc):
            lanes = pl.ds(pl.multiple_of(t * 256, 256), 256)
            depth = pl.ds(pl.multiple_of(h * piece, piece), piece)
            active = jnp.dot(rc[h], wbuf[depth, lanes], preferred_element_type=F32)
            return acc + jnp.sum(cot[:, lanes].astype(F32) * active, axis=1, keepdims=True)
        return lax.fori_loop(0, hidden // 256, active_tile, total)
    gate_grad = lax.fori_loop(0, parts, gate_part, jnp.zeros((cap, 1), F32))
    gate_grad = gate_grad.astype(BF16).astype(F32)
    rows_copy = pltpu.make_async_copy(rc, rows_out, out_sem.at[1])
    rows_copy.start()

    def score_copy(peer):
        return remote(score_src.at[peer], score_dst.at[me], s_send.at[peer], s_recv.at[me], peer)

    def score_arrival(peer):
        return remote(score_src.at[peer], score_dst.at[peer], s_send.at[peer], s_recv.at[peer], peer)

    score_src[...] = jnp.zeros_like(score_src)

    def score_row(i):
        o = lax.rem(me + i, n)
        hit = (picks_col - (o * tok).astype(F32)) == lane
        score_src[o, 0:1, :] = jnp.sum(jnp.where(hit, gate_grad, 0.0), axis=0, keepdims=True)

    def score_send(i):
        score_row(i)
        score_copy(lax.rem(me + i, n)).start()
    loop(1, n, score_send)
    score_row(0)
    score_dst[me] = score_src[me]

    def own_back(h):
        loop(1, plane, lambda i: bwd_arrival(z, h, lax.rem(c + i, plane)).wait_recv())

        @pl.when(z == 0)
        def _():
            zin[z, h] = jnp.zeros(zin.shape[2:], BF16)

        @pl.when(z == nz - 1)
        def _():
            zin[nz, h] = jnp.zeros(zin.shape[2:], BF16)

        @pl.when(z > 0)
        def _():
            remote(zsend.at[z, h], zin.at[z, h], z_send.at[z, h], z_recv.at[z, h], me).wait_recv()

        @pl.when(z < nz - 1)
        def _():
            remote(zsend.at[z, h], zin.at[nz, h], z_send.at[z, h], z_recv.at[nz, h], me).wait_recv()
    loop(1, n, lambda i: score_arrival(lax.rem(me + i, n)).wait_recv())
    score = score_dst[:, 0, :]
    prob = probs[...]
    inner = jnp.sum(prob * score, axis=0, keepdims=True)
    logit_grad = prob * (score - inner)
    logit_col = logit_grad.T.astype(BF16)
    logit_grad = logit_grad.astype(BF16)
    share = width // n
    wide = share % 128 == 0

    def router_tile(t):
        lanes = pl.ds(pl.multiple_of(t * 512, 512), 512)
        part = jnp.dot(logit_grad, tokens[:, lanes], preferred_element_type=F32)
        if wide:
            rs_src[:, lanes] = part
        else:
            rs_src[lanes, :] = part.T
    loop(0, width // 512, router_tile)

    def share_of(d):
        if wide:
            return rs_src.at[:, pl.ds(pl.multiple_of(d * share, share), share)]
        return rs_src.at[pl.ds(pl.multiple_of(d * share, share), share), :]

    def rs_copy(peer):
        return remote(share_of(peer), rs_dst.at[me], r_send.at[peer], r_recv.at[me], peer)

    def rs_arrival(peer):
        return remote(share_of(peer), rs_dst.at[peer], r_send.at[peer], r_recv.at[peer], peer)
    loop(1, n, lambda i: rs_copy(lax.rem(me + i, n)).start())
    rs_dst[me] = share_of(me)[...]

    def final_part(h):
        own_back(h)
        for t in range(piece // tile):
            lanes = slice(t * tile, (t + 1) * tile)
            whole = pl.ds(pl.multiple_of(h * piece + t * tile, tile), tile)
            total = jnp.dot(sel_t[z], bwdbuf[z, h, :, lanes], preferred_element_type=F32)
            total += zin[z, h, :, lanes].astype(F32) + zin[nz, h, :, lanes].astype(F32)
            total += jnp.dot(logit_col, router_t[:, whole], preferred_element_type=F32)
            token_grad[:, whole] = total.astype(BF16)
    loop(0, parts, final_part)

    loop(1, n, lambda i: rs_arrival(lax.rem(me + i, n)).wait_recv())
    total = jnp.sum(rs_dst[...], axis=0)
    router_grad[...] = total.T if wide else total

    def sent(i):
        peer = lax.rem(me + i, n)
        info_copy(peer).wait_send()
        score_copy(peer).wait_send()
        rs_copy(peer).wait_send()
    loop(1, n, sent)

    def sent_plane(k):
        zs = k // (plane * parts)
        h = (k // plane) % parts
        c2 = k % plane

        @pl.when(c2 != c)
        def _():
            fwd_copy(zs, h, c2).wait_send()
            bwd_copy(zs, h, c2).wait_send()
    loop(0, n * parts, sent_plane)

    def sent_z(k):
        zs, h = k // parts, k % parts

        @pl.when((z < nz - 1) & (zs <= z))
        def _():
            token_copy(0, zs, h).wait_send()

        @pl.when((z > 0) & (zs >= z))
        def _():
            token_copy(1, zs, h).wait_send()

        @pl.when(zs != z)
        def _():
            remote(zsend.at[zs, h], zin.at[zs, h], z_send.at[zs, h], z_recv.at[zs, h], me).wait_send()
    loop(0, nz * parts, sent_z)
    scaled_copy.wait()
    rows_copy.wait()


def finish(rows, scaled, token_in, router_in, weight_grad, token_grad, router_grad):
    weight_grad[0] = lax.dot_general(
        rows[0], scaled[...], (((0,), (0,)), ((), ())), preferred_element_type=F32).astype(BF16)
    token_grad[...] = token_in[...]
    router_grad[...] = router_in[...]


def local(tokens, logits, weights, router_weight, expert_picks, cotangent):
    n = lax.axis_size("expert")
    nz = 2 ** math.ceil(math.log2(n) / 3)
    parts = PARTS
    plane = n // nz
    tok, width = tokens.shape
    piece = width // parts
    cap = expert_picks.shape[1]
    hidden = weights.shape[2]
    most = max(2 * cap // n, 16)
    share = width // n
    rs_block = (n, share) if share % 128 == 0 else (share, n)
    rs_full = (n, width) if share % 128 == 0 else (width, n)
    vmem = pl.BlockSpec(memory_space=pltpu.VMEM)
    hbm = pl.BlockSpec(memory_space=pl.ANY)
    dma = pltpu.SemaphoreType.DMA
    flops = 2 * cap * width * hidden * 2
    token_in, rows, scaled, router_in = pl.pallas_call(
        functools.partial(kernel, n, nz, most, parts),
        out_shape=(
            jax.ShapeDtypeStruct((tok, width), BF16),
            jax.ShapeDtypeStruct((parts, cap, piece), BF16),
            jax.ShapeDtypeStruct((cap, hidden), BF16),
            jax.ShapeDtypeStruct((share, n), F32),
        ),
        in_specs=[vmem, vmem, hbm, vmem, vmem, vmem],
        out_specs=(vmem, hbm, hbm, vmem),
        scratch_shapes=[
            pltpu.VMEM((width, hidden), BF16),
            pltpu.VMEM((n, tok), F32),
            pltpu.VMEM((n, 8, 128), F32),
            pltpu.VMEM((n, 8, 128), F32),
            pltpu.VMEM((nz, plane * most, tok), BF16),
            pltpu.VMEM((nz, tok, plane * most), BF16),
            pltpu.VMEM((cap, hidden), BF16),
            pltpu.VMEM((parts, cap, piece), BF16),
            pltpu.VMEM((nz, parts, tok, piece), BF16),
            pltpu.VMEM((nz, parts, plane * most, piece), BF16),
            pltpu.VMEM((parts, n * most, piece), BF16),
            pltpu.VMEM((nz, parts, plane * most, piece), BF16),
            pltpu.VMEM((nz, parts, plane * most, piece), BF16),
            pltpu.VMEM((nz + 1, parts, tok, piece), BF16),
            pltpu.VMEM((nz, parts, tok, piece), BF16),
            pltpu.VMEM((n, 8, 128), F32),
            pltpu.VMEM((n, 8, 128), F32),
            pltpu.VMEM(rs_full, F32),
            pltpu.VMEM((n,) + rs_block, F32),
            dma, dma((2,)),
            dma((n,)), dma((n,)),
            dma((2, nz, parts)), dma((nz, parts)),
            dma((nz, parts, plane)), dma((nz, parts, plane)),
            dma((nz, parts, plane)), dma((nz, parts, plane)),
            dma((nz, parts)), dma((nz + 1, parts)),
            dma((n,)), dma((n,)),
            dma((n,)), dma((n,)),
        ],
        compiler_params=pltpu.CompilerParams(
            collective_id=0, has_side_effects=True, vmem_limit_bytes=62 * 1024 * 1024),
        cost_estimate=pl.CostEstimate(flops=flops, bytes_accessed=8 * 2 ** 20, transcendentals=0),
    )(tokens, logits.T, weights, router_weight.T, expert_picks, cotangent[0])
    block = min(512, piece)
    per = piece // block
    weight_grad, token_grad, router_grad = pl.pallas_call(
        finish,
        grid=(width // block,),
        out_shape=(
            jax.ShapeDtypeStruct((1, width, hidden), BF16),
            jax.ShapeDtypeStruct((tok, width), BF16),
            jax.ShapeDtypeStruct((share, n), F32),
        ),
        in_specs=[
            pl.BlockSpec((1, cap, block), lambda i: (i // per, 0, i % per)),
            pl.BlockSpec((cap, hidden), lambda i: (0, 0)),
            pl.BlockSpec((tok, block), lambda i: (0, i)),
            pl.BlockSpec((share, n), lambda i: (0, 0)),
        ],
        out_specs=(
            pl.BlockSpec((1, block, hidden), lambda i: (0, i, 0)),
            pl.BlockSpec((tok, block), lambda i: (0, i)),
            pl.BlockSpec((share, n), lambda i: (0, 0)),
        ),
        compiler_params=pltpu.CompilerParams(vmem_limit_bytes=32 * 1024 * 1024),
        cost_estimate=pl.CostEstimate(
            flops=flops // 2, bytes_accessed=7 * 2 ** 20, transcendentals=0),
    )(rows, scaled, token_in, router_in)
    return token_grad, weight_grad, router_grad


def solution(mesh):
    in_specs = (
        P(("dp", "expert"), None),
        P(("dp", "expert"), None),
        P("expert", None, None),
        P(),
        P(("dp", "expert"), None),
        P(("dp", "expert"), None, None),
    )
    out_specs = (
        P(("dp", "expert"), None),
        P(("dp", "expert"), None, None),
        P(("dp", "expert"), None),
    )
    return jax.shard_map(local, mesh=mesh, in_specs=in_specs, out_specs=out_specs, check_vma=False)
```

time: 94 us -> 94.8 us (level)
  Pallas kernels: 80.6 us -> 89.1 us
  local copies, waits for them, and re-layouts: 8.83 us -> 4.81 us
  other arithmetic: 3.58 us -> 0 us
    pallas_call x1 -> x2, Pallas kernels: 80.6 us -> 89.1 us  [the longest x1 85.6 us: local(): pl.pallas_call(functools.partial(kernel, n, nz, most, parts), out_shape=(...]
    convert_element_type x2 -> x0, other arithmetic: 2.03 us -> none  [local(): (owner * most + jnp.arange(cap, dtype=jnp.int32) - before).astype(F32)]
    unnamed x2 -> x9, local copies, waits for them, and re-layouts: 6.52 us -> 4.81 us
    pallas_call x1 -> x0, local copies, waits for them, and re-layouts: 1.51 us -> none  [local(): pl.pallas_call(functools.partial(kernel, n, nz, most), out_shape=(jax.Sha...]
where the time goes in v2:
time: 94.8 us; the launch traced here: 94.5 us
  Pallas kernels  89.1 us (94%)
  local copies, waits for them, and re-layouts  4.81 us (5%)
    pallas_call x1, Pallas kernels, local(): pl.pallas_call(functools.partial(kernel, n, nz, most, parts), out_shape=(...  85.6 us
    unnamed x9, local copies, waits for them, and re-layouts  4.81 us
    pallas_call x1, Pallas kernels, local(): pl.pallas_call(finish, grid=(width // block,), out_shape=(jax.ShapeDtypeS...  3.48 us

profile of v2, /device:TPU:0, one launch (start us, length us, event | category | flops | bytes accessed | tf_op | source)
XLA Modules:
  0.0 94.5 jit_solution(13713291195315600168)
XLA Ops:
  0.6 85.6 %shard_map.85 = (bf16[128,2048]{1,0:T(8,128)(2,1)}, bf16[2,256,1024]{2,1,0:T(8,128)(2,1)}, bf16[256,1024]{1,0:T(8,128)(2,1)}, f32[128,16]{1,0:T(8,128)}) custom-call(bf16[128,2048]{1,0:T(8,128)(2,1)} %tokens.1, f32[16,128]{1,0:T(8,128)} %bitcast.5, bf16[1,2048,1024]{2,1,0:T(8,128)(2,1)} %weights.1, bf16[16,2048]{1,0:T(8,128)(2,1)} %bitcast.4, ...), custom_call_target="tpu_custom_call" | custom-call | flops 2147483648 | bytes 8388608 | tf_op jit(solution)/shard_map/pallas_call | solution.py:437
  86.2 0.0 copy-start
  86.2 1.2 %copy-done = bf16[2,256,1024]{2,1,0:T(8,128)(2,1)S(1)} copy-done((bf16[2,256,1024]{2,1,0:T(8,128)(2,1)S(1)}, bf16[2,256,1024]{2,1,0:T(8,128)(2,1)}, u32[]{:S(2)}) %copy-start) | copy-done | bytes 1048600
  87.5 0.0 copy-start.1
  87.5 1.0 %copy-done.1 = bf16[128,2048]{1,0:T(8,128)(2,1)S(1)} copy-done((bf16[128,2048]{1,0:T(8,128)(2,1)S(1)}, bf16[128,2048]{1,0:T(8,128)(2,1)}, u32[]{:S(2)}) %copy-start.1) | copy-done | bytes 524312
  88.5 0.0 copy-start.2
  88.5 1.0 %copy-done.2 = bf16[256,1024]{1,0:T(8,128)(2,1)S(1)} copy-done((bf16[256,1024]{1,0:T(8,128)(2,1)S(1)}, bf16[256,1024]{1,0:T(8,128)(2,1)}, u32[]{:S(2)}) %copy-start.2) | copy-done | bytes 524312
  89.5 0.0 copy-start.3
  89.5 0.8 copy-done.3
  90.4 3.5 %shard_map.86 = (bf16[1,2048,1024]{2,1,0:T(8,128)(2,1)}, bf16[128,2048]{1,0:T(8,128)(2,1)}, f32[128,16]{1,0:T(8,128)S(1)}) custom-call(bf16[2,256,1024]{2,1,0:T(8,128)(2,1)S(1)} %copy-done, bf16[256,1024]{1,0:T(8,128)(2,1)S(1)} %copy-done.2, bf16[128,2048]{1,0:T(8,128)(2,1)S(1)} %copy-done.1, f32[128,16]{1,0:T(8,128)S(1)} %copy-done.3), custom_call_target="tpu_custom_call" | custom-call | flops 1073741824 | bytes 7340032 | tf_op jit(solution)/shard_map/pallas_call | solution.py:482
  93.9 0.7 copy.9
Async XLA Ops:
  86.2 1.2 %copy-start = (bf16[2,256,1024]{2,1,0:T(8,128)(2,1)S(1)}, bf16[2,256,1024]{2,1,0:T(8,128)(2,1)}, u32[]{:S(2)}) copy-start(bf16[2,256,1024]{2,1,0:T(8,128)(2,1)} %get-tuple-element.10.rows) | copy-start | bytes 3145732
  87.5 1.0 %copy-start.1 = (bf16[128,2048]{1,0:T(8,128)(2,1)S(1)}, bf16[128,2048]{1,0:T(8,128)(2,1)}, u32[]{:S(2)}) copy-start(bf16[128,2048]{1,0:T(8,128)(2,1)} %get-tuple-element.12.token_in) | copy-start | bytes 1572868
  88.5 1.0 %copy-start.2 = (bf16[256,1024]{1,0:T(8,128)(2,1)S(1)}, bf16[256,1024]{1,0:T(8,128)(2,1)}, u32[]{:S(2)}) copy-start(bf16[256,1024]{1,0:T(8,128)(2,1)} %get-tuple-element.11.scaled) | copy-start | bytes 1572868
  89.5 0.8 copy-start.3

commit v3 on v2

--- a/solution.py
+++ b/solution.py
@@ -168,8 +168,8 @@
                 backward(dest, h)
         loop(0, 2, one)
 
-    ahead = parts
-    loop(0, ahead, backward_at)
+    late = parts + 1
+    loop(0, parts, backward_at)
 
     tok_col = lax.broadcasted_iota(jnp.int32, (tok, 128), 0).astype(F32)
     slot_lane = lax.broadcasted_iota(jnp.int32, (tok, group), 1).astype(F32)
@@ -251,13 +251,13 @@
 
     def substep(q):
         loop(0, 2, lambda way: forward_at(q, way))
-        backward_at(q + ahead)
+        backward_at(q + parts)
 
         @pl.when((q >= parts * (nz - 2)) & (q < parts * (nz - 1)))
         def _():
             backward(z, q % parts)
-        loop(0, 2, lambda way: chain_at(q, way))
-    loop(0, nz * parts, substep)
+        loop(0, 2, lambda way: chain_at(q - late, way))
+    loop(0, nz * parts + late, substep)
 
     slot_lanes = lax.broadcasted_iota(jnp.int32, (cap, n * most), 1).astype(F32)
     compact = jnp.where(slot_lanes == placed_col, 1.0, 0.0).astype(BF16)
@@ -371,7 +371,7 @@
 
     loop(1, n, lambda i: rs_arrival(lax.rem(me + i, n)).wait_recv())
     total = jnp.sum(rs_dst[...], axis=0)
-    router_grad[...] = total.T if wide else total
+    router_grad[...] = total
 
     def sent(i):
         peer = lax.rem(me + i, n)
@@ -440,7 +440,7 @@
             jax.ShapeDtypeStruct((tok, width), BF16),
             jax.ShapeDtypeStruct((parts, cap, piece), BF16),
             jax.ShapeDtypeStruct((cap, hidden), BF16),
-            jax.ShapeDtypeStruct((share, n), F32),
+            jax.ShapeDtypeStruct(rs_block, F32),
         ),
         in_specs=[vmem, vmem, hbm, vmem, vmem, vmem],
         out_specs=(vmem, hbm, hbm, vmem),
@@ -485,24 +485,24 @@
         out_shape=(
             jax.ShapeDtypeStruct((1, width, hidden), BF16),
             jax.ShapeDtypeStruct((tok, width), BF16),
-            jax.ShapeDtypeStruct((share, n), F32),
+            jax.ShapeDtypeStruct(rs_block, F32),
         ),
         in_specs=[
             pl.BlockSpec((1, cap, block), lambda i: (i // per, 0, i % per)),
             pl.BlockSpec((cap, hidden), lambda i: (0, 0)),
             pl.BlockSpec((tok, block), lambda i: (0, i)),
-            pl.BlockSpec((share, n), lambda i: (0, 0)),
+            pl.BlockSpec(rs_block, lambda i: (0, 0)),
         ],
         out_specs=(
             pl.BlockSpec((1, block, hidden), lambda i: (0, i, 0)),
             pl.BlockSpec((tok, block), lambda i: (0, i)),
-            pl.BlockSpec((share, n), lambda i: (0, 0)),
+            pl.BlockSpec(rs_block, lambda i: (0, 0)),
         ),
-        compiler_params=pltpu.CompilerParams(vmem_limit_bytes=32 * 1024 * 1024),
+        compiler_params=pltpu.CompilerParams(vmem_limit_bytes=62 * 1024 * 1024),
         cost_estimate=pl.CostEstimate(
             flops=flops // 2, bytes_accessed=7 * 2 ** 20, transcendentals=0),
     )(rows, scaled, token_in, router_in)
-    return token_grad, weight_grad, router_grad
+    return token_grad, weight_grad, router_grad.T if share % 128 == 0 else router_grad
 
 
 def solution(mesh):

time: 94.8 us -> 86.3 us (0.910)
  local copies, waits for them, and re-layouts: 4.81 us -> 0 us
  Pallas kernels: 89.1 us -> 85.4 us
    pallas_call x1, Pallas kernels: 85.6 us -> 80.3 us  [local(): pl.pallas_call(functools.partial(kernel, n, nz, most, parts), out_shape=(...]
    unnamed x9 -> x0, local copies, waits for them, and re-layouts: 4.81 us -> none
    pallas_call x1, Pallas kernels: 3.48 us -> 5.12 us  [local(): pl.pallas_call(finish, grid=(width // block,), out_shape=(jax.ShapeDtypeS...]
where the time goes in v3:
time: 86.3 us; the launch traced here: 86.1 us
  Pallas kernels  85.4 us (99%)
    pallas_call x1, Pallas kernels, local(): pl.pallas_call(functools.partial(kernel, n, nz, most, parts), out_shape=(...  80.3 us
    pallas_call x1, Pallas kernels, local(): pl.pallas_call(finish, grid=(width // block,), out_shape=(jax.ShapeDtypeS...  5.12 us

profile of v3, /device:TPU:0, one launch (start us, length us, event | category | flops | bytes accessed | tf_op | source)
XLA Modules:
  0.0 86.1 jit_solution(7445625285444675517)
XLA Ops:
  0.6 80.3 %shard_map.85 = (bf16[128,2048]{1,0:T(8,128)(2,1)}, bf16[2,256,1024]{2,1,0:T(8,128)(2,1)}, bf16[256,1024]{1,0:T(8,128)(2,1)}, f32[16,128]{1,0:T(8,128)}) custom-call(bf16[128,2048]{1,0:T(8,128)(2,1)} %tokens.1, f32[16,128]{1,0:T(8,128)} %bitcast.6, bf16[1,2048,1024]{2,1,0:T(8,128)(2,1)} %weights.1, bf16[16,2048]{1,0:T(8,128)(2,1)} %bitcast.5, ...), custom_call_target="tpu_custom_call" | custom-call | flops 2147483648 | bytes 8388608 | tf_op jit(solution)/shard_map/pallas_call | solution.py:437
  81.0 5.1 %shard_map.86 = (bf16[1,2048,1024]{2,1,0:T(8,128)(2,1)}, bf16[128,2048]{1,0:T(8,128)(2,1)}, f32[16,128]{1,0:T(8,128)}) custom-call(bf16[2,256,1024]{2,1,0:T(8,128)(2,1)} %get-tuple-element.10.rows, bf16[256,1024]{1,0:T(8,128)(2,1)} %get-tuple-element.11.scaled, bf16[128,2048]{1,0:T(8,128)(2,1)} %get-tuple-element.12.token_in, ...), custom_call_target="tpu_custom_call" | custom-call | flops 1073741824 | bytes 7340032 | tf_op jit(solution)/shard_map/pallas_call | solution.py:482

commit v4 on v3

--- a/solution.py
+++ b/solution.py
@@ -107,69 +107,8 @@
     loop(0, 2 * parts, token_start)
     loop(1, n, lambda i: info_arrival(lax.rem(me + i, n)).wait_recv())
 
-    lane = lax.broadcasted_iota(jnp.int32, (cap, 128), 1).astype(F32)
-
-    def add_gate(o, acc):
-        hit = (picks_col - (o * tok).astype(F32)) == lane
-        return acc + jnp.where(hit, info_dst[o, 0:1, :], 0.0)
-    gate = jnp.sum(lax.fori_loop(0, n, add_gate, jnp.zeros((cap, 128), F32)), axis=1, keepdims=True)
-    gate = gate.astype(BF16).astype(F32)
-    scaled[...] = (gate * cot[...].astype(F32)).astype(BF16)
-    scaled_copy = pltpu.make_async_copy(scaled, scaled_out, out_sem.at[0])
-    scaled_copy.start()
-    w_copy.wait()
-
-    def row_tile(t):
-        rows = pl.ds(pl.multiple_of(t * tile, tile), tile)
-        per = piece // tile
-        lanes = pl.ds(pl.multiple_of((t % per) * tile, tile), tile)
-        rg[t // per, :, lanes] = lax.dot_general(
-            scaled[...], wbuf[rows, :], (((1,), (1,)), ((), ())),
-            preferred_element_type=F32).astype(BF16)
-    loop(0, width // tile, row_tile)
-
     def mine_of(c2):
         return pl.ds(pl.multiple_of(c2 * most, most), most)
-
-    def bwd_copy(zd, h, c2):
-        return remote(bwd_src.at[zd, h, mine_of(c2), :], bwdbuf.at[zd, h, mine_of(c), :],
-                      b_send.at[zd, h, c2], b_recv.at[zd, h, c], z * plane + c2)
-
-    def bwd_arrival(zd, h, c2):
-        return remote(bwd_src.at[zd, h, mine_of(c2), :], bwdbuf.at[zd, h, mine_of(c2), :],
-                      b_send.at[zd, h, c2], b_recv.at[zd, h, c2], z * plane + c2)
-
-    slot_row = lax.broadcasted_iota(jnp.int32, (group, cap), 0).astype(F32)
-
-    def backward(zd, h):
-        low = (zd * group).astype(F32)
-        spread = jnp.where(slot_row == placed_row - low, 1.0, 0.0).astype(BF16)
-        for t in range(piece // tile):
-            lanes = slice(t * tile, (t + 1) * tile)
-            bwd_src[zd, h, :, lanes] = jnp.dot(
-                spread, rg[h, :, lanes], preferred_element_type=F32).astype(BF16)
-        loop(1, plane, lambda i: bwd_copy(zd, h, lax.rem(c + i, plane)).start())
-        bwdbuf[zd, h, mine_of(c), :] = bwd_src[zd, h, mine_of(c), :]
-
-    def chain_place(q, way):
-        start = jnp.where(way == 0, z, nz - 1 - z)
-        k = q - start
-        block = jnp.maximum(k, 0) // parts
-        dest = jnp.where(way == 0, nz - 1 - block, block)
-        valid = (k >= 0) & (block < nz - 1 - start)
-        return valid, jnp.minimum(jnp.maximum(dest, 0), nz - 1), jnp.maximum(k, 0) % parts, start > 0
-
-    def backward_at(q):
-        def one(way):
-            valid, dest, h, _ = chain_place(q, way)
-
-            @pl.when(valid)
-            def _():
-                backward(dest, h)
-        loop(0, 2, one)
-
-    late = parts + 1
-    loop(0, parts, backward_at)
 
     tok_col = lax.broadcasted_iota(jnp.int32, (tok, 128), 0).astype(F32)
     slot_lane = lax.broadcasted_iota(jnp.int32, (tok, group), 1).astype(F32)
@@ -192,7 +131,6 @@
         made = lax.fori_loop(0, plane, one, jnp.zeros((tok, group), F32))
         sel_t[zs] = made.astype(BF16)
         sel[zs] = made.T.astype(BF16)
-    loop(0, nz, build_sel)
 
     def rows_of(zs, c2):
         return pl.ds(pl.multiple_of((zs * plane + c2) * most, most), most)
@@ -205,25 +143,92 @@
         return remote(fwd_src.at[zs, h, mine_of(c2), :], rowbuf.at[h, rows_of(zs, c2), :],
                       f_send.at[zs, h, c2], f_recv.at[zs, h, c2], z * plane + c2)
 
+    def pick_rows(src, h):
+        for t in range(piece // tile):
+            lanes = slice(t * tile, (t + 1) * tile)
+            fwd_src[src, h, :, lanes] = jnp.dot(
+                sel[src], tokbuf[src, h, :, lanes], preferred_element_type=F32).astype(BF16)
+        loop(1, plane, lambda i: fwd_copy(src, h, lax.rem(c + i, plane)).start())
+        rowbuf[h, rows_of(src, c), :] = fwd_src[src, h, mine_of(c), :]
+
+    build_sel(z)
+    loop(0, parts, lambda h: pick_rows(z, h))
+
+    lane = lax.broadcasted_iota(jnp.int32, (cap, 128), 1).astype(F32)
+
+    def add_gate(o, acc):
+        hit = (picks_col - (o * tok).astype(F32)) == lane
+        return acc + jnp.where(hit, info_dst[o, 0:1, :], 0.0)
+    gate = jnp.sum(lax.fori_loop(0, n, add_gate, jnp.zeros((cap, 128), F32)), axis=1, keepdims=True)
+    gate = gate.astype(BF16).astype(F32)
+    scaled[...] = (gate * cot[...].astype(F32)).astype(BF16)
+    scaled_copy = pltpu.make_async_copy(scaled, scaled_out, out_sem.at[0])
+    scaled_copy.start()
+    w_copy.wait()
+
+    def row_tile(t):
+        rows = pl.ds(pl.multiple_of(t * tile, tile), tile)
+        per = piece // tile
+        lanes = pl.ds(pl.multiple_of((t % per) * tile, tile), tile)
+        rg[t // per, :, lanes] = lax.dot_general(
+            scaled[...], wbuf[rows, :], (((1,), (1,)), ((), ())),
+            preferred_element_type=F32).astype(BF16)
+    loop(0, width // tile, row_tile)
+
+    def bwd_copy(zd, h, c2):
+        return remote(bwd_src.at[zd, h, mine_of(c2), :], bwdbuf.at[zd, h, mine_of(c), :],
+                      b_send.at[zd, h, c2], b_recv.at[zd, h, c], z * plane + c2)
+
+    def bwd_arrival(zd, h, c2):
+        return remote(bwd_src.at[zd, h, mine_of(c2), :], bwdbuf.at[zd, h, mine_of(c2), :],
+                      b_send.at[zd, h, c2], b_recv.at[zd, h, c2], z * plane + c2)
+
+    slot_row = lax.broadcasted_iota(jnp.int32, (group, cap), 0).astype(F32)
+
+    def backward(zd, h):
+        low = (zd * group).astype(F32)
+        spread = jnp.where(slot_row == placed_row - low, 1.0, 0.0).astype(BF16)
+        for t in range(piece // tile):
+            lanes = slice(t * tile, (t + 1) * tile)
+            bwd_src[zd, h, :, lanes] = jnp.dot(
+                spread, rg[h, :, lanes], preferred_element_type=F32).astype(BF16)
+        loop(1, plane, lambda i: bwd_copy(zd, h, lax.rem(c + i, plane)).start())
+        bwdbuf[zd, h, mine_of(c), :] = bwd_src[zd, h, mine_of(c), :]
+
+    def chain_place(q, way):
+        start = jnp.where(way == 0, z, nz - 1 - z)
+        k = q - start
+        block = jnp.maximum(k, 0) // parts
+        dest = jnp.where(way == 0, nz - 1 - block, block)
+        valid = (k >= 0) & (block < nz - 1 - start)
+        return valid, jnp.minimum(jnp.maximum(dest, 0), nz - 1), jnp.maximum(k, 0) % parts, start > 0
+
+    def backward_at(q):
+        def one(way):
+            valid, dest, h, _ = chain_place(q, way)
+
+            @pl.when(valid)
+            def _():
+                backward(dest, h)
+        loop(0, 2, one)
+
+    late = parts + 1
+    loop(0, parts, backward_at)
+
+    loop(1, nz, lambda k: build_sel(lax.rem(z + k, nz)))
+
     def forward_at(q, way):
         far, h = q // parts, q % parts
         src = z + (2 * way - 1) * far
 
-        @pl.when((src >= 0) & (src < nz) & ((far > 0) | (way == 0)))
-        def _():
-            @pl.when(far > 0)
+        @pl.when((src >= 0) & (src < nz) & (far > 0))
+        def _():
+            token_copy(way, src, h).wait_recv()
+
+            @pl.when(goes_on(way))
             def _():
-                token_copy(way, src, h).wait_recv()
-
-                @pl.when(goes_on(way))
-                def _():
-                    token_copy(way, src, h).start()
-            for t in range(piece // tile):
-                lanes = slice(t * tile, (t + 1) * tile)
-                fwd_src[src, h, :, lanes] = jnp.dot(
-                    sel[src], tokbuf[src, h, :, lanes], preferred_element_type=F32).astype(BF16)
-            loop(1, plane, lambda i: fwd_copy(src, h, lax.rem(c + i, plane)).start())
-            rowbuf[h, rows_of(src, c), :] = fwd_src[src, h, mine_of(c), :]
+                token_copy(way, src, h).start()
+            pick_rows(src, h)
 
     def chain_at(q, way):
         valid, dest, h, has_in = chain_place(q, way)
@@ -253,9 +258,9 @@
         loop(0, 2, lambda way: forward_at(q, way))
         backward_at(q + parts)
 
-        @pl.when((q >= parts * (nz - 2)) & (q < parts * (nz - 1)))
-        def _():
-            backward(z, q % parts)
+        @pl.when((q >= parts * nz - 1) & (q < parts * nz + parts - 1))
+        def _():
+            backward(z, q - (parts * nz - 1))
         loop(0, 2, lambda way: chain_at(q - late, way))
     loop(0, nz * parts + late, substep)
 

time: 86.3 us -> 78.1 us (0.905)
  Pallas kernels: 85.4 us -> 77.2 us
    pallas_call x1, Pallas kernels: 80.3 us -> 72.1 us  [local(): pl.pallas_call(functools.partial(kernel, n, nz, most, parts), out_shape=(...]
where the time goes in v4:
time: 78.1 us; the launch traced here: 77.9 us
  Pallas kernels  77.2 us (99%)
    pallas_call x1, Pallas kernels, local(): pl.pallas_call(functools.partial(kernel, n, nz, most, parts), out_shape=(...  72.1 us
    pallas_call x1, Pallas kernels, local(): pl.pallas_call(finish, grid=(width // block,), out_shape=(jax.ShapeDtypeS...  5.12 us

profile of v4, /device:TPU:0, one launch (start us, length us, event | category | flops | bytes accessed | tf_op | source)
XLA Modules:
  0.0 77.9 jit_solution(4246157774764157466)
XLA Ops:
  0.6 72.1 %shard_map.85 = (bf16[128,2048]{1,0:T(8,128)(2,1)}, bf16[2,256,1024]{2,1,0:T(8,128)(2,1)}, bf16[256,1024]{1,0:T(8,128)(2,1)}, f32[16,128]{1,0:T(8,128)}) custom-call(bf16[128,2048]{1,0:T(8,128)(2,1)} %tokens.1, f32[16,128]{1,0:T(8,128)} %bitcast.6, bf16[1,2048,1024]{2,1,0:T(8,128)(2,1)} %weights.1, bf16[16,2048]{1,0:T(8,128)(2,1)} %bitcast.5, ...), custom_call_target="tpu_custom_call" | custom-call | flops 2147483648 | bytes 8388608 | tf_op jit(solution)/shard_map/pallas_call | solution.py:442
  72.7 5.1 %shard_map.86 = (bf16[1,2048,1024]{2,1,0:T(8,128)(2,1)}, bf16[128,2048]{1,0:T(8,128)(2,1)}, f32[16,128]{1,0:T(8,128)}) custom-call(bf16[2,256,1024]{2,1,0:T(8,128)(2,1)} %get-tuple-element.10.rows, bf16[256,1024]{1,0:T(8,128)(2,1)} %get-tuple-element.11.scaled, bf16[128,2048]{1,0:T(8,128)(2,1)} %get-tuple-element.12.token_in, ...), custom_call_target="tpu_custom_call" | custom-call | flops 1073741824 | bytes 7340032 | tf_op jit(solution)/shard_map/pallas_call | solution.py:487

commit v5 on v4

--- a/solution.py
+++ b/solution.py
@@ -256,7 +256,11 @@
 
     def substep(q):
         loop(0, 2, lambda way: forward_at(q, way))
-        backward_at(q + parts)
+
+        @pl.when(q >= parts)
+        def _():
+            backward_at(q)
+
 
         @pl.when((q >= parts * nz - 1) & (q < parts * nz + parts - 1))
         def _():

time: 78.1 us -> 78.1 us (level)
  no operation moved by 1% of the time
where the time goes in v5:
time: 78.1 us; the launch traced here: 77.9 us
  Pallas kernels  77.3 us (99%)
    pallas_call x1, Pallas kernels, local(): pl.pallas_call(functools.partial(kernel, n, nz, most, parts), out_shape=(...  72.1 us
    pallas_call x1, Pallas kernels, local(): pl.pallas_call(finish, grid=(width // block,), out_shape=(jax.ShapeDtypeS...  5.12 us

profile of v5, /device:TPU:0, one launch (start us, length us, event | category | flops | bytes accessed | tf_op | source)
XLA Modules:
  0.0 77.9 jit_solution(12778100382164810685)
XLA Ops:
  0.6 72.1 %shard_map.85 = (bf16[128,2048]{1,0:T(8,128)(2,1)}, bf16[2,256,1024]{2,1,0:T(8,128)(2,1)}, bf16[256,1024]{1,0:T(8,128)(2,1)}, f32[16,128]{1,0:T(8,128)}) custom-call(bf16[128,2048]{1,0:T(8,128)(2,1)} %tokens.1, f32[16,128]{1,0:T(8,128)} %bitcast.6, bf16[1,2048,1024]{2,1,0:T(8,128)(2,1)} %weights.1, bf16[16,2048]{1,0:T(8,128)(2,1)} %bitcast.5, ...), custom_call_target="tpu_custom_call" | custom-call | flops 2147483648 | bytes 8388608 | tf_op jit(solution)/shard_map/pallas_call | solution.py:446
  72.8 5.1 %shard_map.86 = (bf16[1,2048,1024]{2,1,0:T(8,128)(2,1)}, bf16[128,2048]{1,0:T(8,128)(2,1)}, f32[16,128]{1,0:T(8,128)}) custom-call(bf16[2,256,1024]{2,1,0:T(8,128)(2,1)} %get-tuple-element.10.rows, bf16[256,1024]{1,0:T(8,128)(2,1)} %get-tuple-element.11.scaled, bf16[128,2048]{1,0:T(8,128)(2,1)} %get-tuple-element.12.token_in, ...), custom_call_target="tpu_custom_call" | custom-call | flops 1073741824 | bytes 7340032 | tf_op jit(solution)/shard_map/pallas_call | solution.py:491

commit v6 on v5

--- a/solution.py
+++ b/solution.py
@@ -89,7 +89,7 @@
     loop(1, n, lambda i: info_copy(lax.rem(me + i, n)).start())
 
     def next_of(way):
-        return me + plane * (1 - 2 * way)
+        return lax.rem(me + plane * (1 - 2 * way) + n, n)
 
     def goes_on(way):
         return jnp.where(way == 0, z < nz - 1, z > 0)
@@ -486,7 +486,7 @@
             collective_id=0, has_side_effects=True, vmem_limit_bytes=62 * 1024 * 1024),
         cost_estimate=pl.CostEstimate(flops=flops, bytes_accessed=8 * 2 ** 20, transcendentals=0),
     )(tokens, logits.T, weights, router_weight.T, expert_picks, cotangent[0])
-    block = min(512, piece)
+    block = min(256, piece)
     per = piece // block
     weight_grad, token_grad, router_grad = pl.pallas_call(
         finish,

time: 78.1 us -> 80.3 us (1.028)
  Pallas kernels: 77.3 us -> 79.4 us
    pallas_call x1, Pallas kernels: 5.12 us -> 7.26 us  [local(): pl.pallas_call(finish, grid=(width // block,), out_shape=(jax.ShapeDtypeS...]
where the time goes in v6:
time: 80.3 us; the launch traced here: 80 us
  Pallas kernels  79.4 us (99%)
    pallas_call x1, Pallas kernels, local(): pl.pallas_call(functools.partial(kernel, n, nz, most, parts), out_shape=(...  72.1 us
    pallas_call x1, Pallas kernels, local(): pl.pallas_call(finish, grid=(width // block,), out_shape=(jax.ShapeDtypeS...  7.26 us

profile of v6, /device:TPU:0, one launch (start us, length us, event | category | flops | bytes accessed | tf_op | source)
XLA Modules:
  0.0 80.0 jit_solution(13123139327857620018)
XLA Ops:
  0.6 72.1 %shard_map.85 = (bf16[128,2048]{1,0:T(8,128)(2,1)}, bf16[2,256,1024]{2,1,0:T(8,128)(2,1)}, bf16[256,1024]{1,0:T(8,128)(2,1)}, f32[16,128]{1,0:T(8,128)}) custom-call(bf16[128,2048]{1,0:T(8,128)(2,1)} %tokens.1, f32[16,128]{1,0:T(8,128)} %bitcast.6, bf16[1,2048,1024]{2,1,0:T(8,128)(2,1)} %weights.1, bf16[16,2048]{1,0:T(8,128)(2,1)} %bitcast.5, ...), custom_call_target="tpu_custom_call" | custom-call | flops 2147483648 | bytes 8388608 | tf_op jit(solution)/shard_map/pallas_call | solution.py:446
  72.8 7.3 %shard_map.86 = (bf16[1,2048,1024]{2,1,0:T(8,128)(2,1)}, bf16[128,2048]{1,0:T(8,128)(2,1)}, f32[16,128]{1,0:T(8,128)}) custom-call(bf16[2,256,1024]{2,1,0:T(8,128)(2,1)} %get-tuple-element.10.rows, bf16[256,1024]{1,0:T(8,128)(2,1)} %get-tuple-element.11.scaled, bf16[128,2048]{1,0:T(8,128)(2,1)} %get-tuple-element.12.token_in, ...), custom_call_target="tpu_custom_call" | custom-call | flops 1073741824 | bytes 7340032 | tf_op jit(solution)/shard_map/pallas_call | solution.py:491
